TPU v7x, 256 devices: a whole 4x4x8 slice. The times are simulated.
256 devices in a mesh: rep: 4 (over z_hi), fsdp: 64 (over z_lo, y, x, core).
Axes of the slice: x: 4, y: 4, z: 8 (z_hi: 4, z_lo: 2; z = z_hi * 2 + z_lo), core: 2. Of those that a mesh axis runs over, the one named last changes fastest.
Arguments:
- inputs: bfloat16 [4, 12288, 4096], P('rep', 'fsdp'), may hold values from -16 to 16
- grad_kv: bfloat16 [4, 12288, 1024], P('rep', 'fsdp'), may hold values from -6 to 6
- local_weight: float32 [4, 4096, 1024], P('rep', 'fsdp'), may hold values from -0.09375 to 0.09375
- global_weight: float32 [4096, 1024], P('fsdp'), may hold values from -0.09375 to 0.09375
- outer_moment: float32 [4096, 1024], P('fsdp'), may hold values from -0.15625 to 0.15625
- arrived: float32 [4096, 512], P('fsdp'), may hold values from -0.09375 to 0.09375
- fragment: int32 [1], replicated, may hold values from 0 to 65535
Outputs:
- keys_values: bfloat16 [4, 12288, 1024], P('rep', 'fsdp')
- grad_input: bfloat16 [4, 12288, 4096], P('rep', 'fsdp')
- local_next: float32 [4, 4096, 1024], P('rep', 'fsdp')
- global_next: float32 [4096, 1024], P('fsdp')
- moment_next: float32 [4096, 1024], P('fsdp')
Inputs may be any that keep to these rules, and one draw needn't show every extreme that they name: `fragment`: an even number names the key columns, an odd one the value columns.
All inputs are finite; a program needn't handle non-finite values.
Results may differ from a plain program's by a relative error of at most 0.001.
The roundings to bfloat16 on the way count: a program that leaves them out, or rounds other values in their place, can miss the bound.
Values may be sent and summed in bfloat16 or wider, within the bound.
A program may use at most 128 MiB of HBM per device.

v0:
```python
import jax
import jax.numpy as jnp
from jax import lax
from jax.sharding import PartitionSpec as P

inner_rate = 0.0001
outer_rate = 0.7
moment_keep = 0.9
merge_keep = 0.5


def nesterov(delta_sum, global_part, moment_part, replicas):
    mean_delta = delta_sum / replicas
    moment_new = moment_keep * moment_part + mean_delta
    global_new = global_part - outer_rate * (mean_delta + moment_keep * moment_new)
    return (global_new, moment_new)


def local(inputs, grad_kv, local_weight, global_weight, outer_moment, arrived, fragment):
    rows = inputs[0]
    cotangent = grad_kv[0]
    weight = local_weight[0]
    weight_bf = weight.astype(jnp.bfloat16)
    width = arrived.shape[1]
    contract_cols = (((1,), (1,)), ((), ()))
    contract_rows = (((0,), (0,)), ((), ()))
    full_weight = lax.all_gather(weight_bf, "fsdp", axis=0, tiled=True)
    produced = jnp.dot(rows, full_weight, preferred_element_type=jnp.float32)
    back = lax.dot_general(
        cotangent, full_weight, contract_cols, preferred_element_type=jnp.float32
    )
    gradient = lax.psum_scatter(
        lax.dot_general(rows, cotangent, contract_rows, preferred_element_type=jnp.float32),
        "fsdp",
        scatter_dimension=0,
        tiled=True,
    )
    inner = weight - inner_rate * gradient
    start = fragment[0] % 2 * width
    zero = jnp.int32(0)
    local_part = lax.dynamic_slice_in_dim(weight, start, width, 1)
    global_part = lax.dynamic_slice_in_dim(global_weight, start, width, 1)
    moment_part = lax.dynamic_slice_in_dim(outer_moment, start, width, 1)
    delta = global_part - local_part
    replicas = lax.axis_size("rep")
    delta_sum = lax.psum(delta, "rep")
    global_new, moment_new = nesterov(delta_sum, global_part, moment_part, replicas)
    moment_next = lax.dynamic_update_slice(outer_moment, moment_new, (zero, start))
    global_next = lax.dynamic_update_slice(global_weight, global_new, (zero, start))
    inner_part = lax.dynamic_slice_in_dim(inner, start, width, 1)
    merged = merge_keep * inner_part + (1.0 - merge_keep) * arrived
    local_next = lax.dynamic_update_slice(inner, merged, (zero, start))
    return (
        produced.astype(jnp.bfloat16)[None],
        back.astype(jnp.bfloat16)[None],
        local_next[None],
        global_next,
        moment_next,
    )


def solution(mesh):
    return jax.shard_map(
        local,
        mesh=mesh,
        in_specs=(
            P("rep", "fsdp", None),
            P("rep", "fsdp", None),
            P("rep", "fsdp", None),
            P("fsdp", None),
            P("fsdp", None),
            P("fsdp", None),
            P(),
        ),
        out_specs=(
            P("rep", "fsdp", None),
            P("rep", "fsdp", None),
            P("rep", "fsdp", None),
            P("fsdp", None),
            P("fsdp", None),
        ),
        check_vma=False,
    )
```

profile of v0, /device:TPU:1, one launch (start us, length us, event | category | flops | bytes accessed | tf_op | source)
XLA Modules:
  0.0 451.7 jit_solution(1754891539745619062)
XLA Ops:
  8.0 0.0 copy-start
  8.0 0.0 all-reduce.2.cloned.1.call-start
  8.1 1.1 copy.19
  9.8 1.6 bitcast_subtract_fusion.1
  11.4 0.0 all-reduce.2.cloned.1.call-update
  11.4 0.0 all-gather.2.cloned.1.call-start
  11.4 1.6 bitcast_convert_fusion
  13.1 0.0 all-gather.2.cloned.1.call-update
  13.1 0.0 reduce-scatter.2.cloned.1.call-start
  13.2 9.1 %fusion.1 = f32[4096,1024]{1,0:T(8,128)} fusion(bf16[1,192,4096]{2,1,0:T(8,128)(2,1)S(1)} %copy-done, bf16[1,192,1024]{2,1,0:T(8,128)(2,1)} %param.8), kind=kOutput, calls=%fused_computation.2 | convolution fusion | flops 1610612736 | bytes 18743296 | tf_op jit(solution)/shard_map/dot_general | solution.py:33
  22.3 0.0 reduce-scatter.2.cloned.1.call-update
  22.3 41.4 %all-reduce.2.cloned.1.call-done = f32[64,512]{1,0:T(8,128)} async-done(((f32[64,512]{1,0:T(8,128)}), f32[64,512]{1,0:T(8,128)}) %all-reduce.2.cloned.1.call-update) | async-done | bytes 131088 | tf_op jit(solution)/shard_map/psum | solution.py:46
  63.7 1.0 fusion.13
  64.6 0.0 copy-start.2
  64.6 0.0 copy-start.3
  64.7 68.0 %all-gather.2.cloned.1.call-done = bf16[4096,1024]{1,0:T(8,128)(2,1)} async-done(((bf16[64,1024]{1,0:T(8,128)(2,1)}), bf16[4096,1024]{1,0:T(8,128)(2,1)}) %all-gather.2.cloned.1.call-update) | async-done | bytes 8388624 | tf_op jit(solution)/shard_map/all_gather | solution.py:27
  132.6 7.6 %fusion = bf16[1,192,4096]{2,1,0:T(8,128)(2,1)} fusion(bf16[4096,1024]{1,0:T(8,128)(2,1)} %all-gather.2.cloned.1.call-done, bf16[1,192,1024]{2,1,0:T(8,128)(2,1)S(1)} %copy-done.5), kind=kOutput, calls=%fused_computation.1 | convolution fusion | flops 1611399168 | bytes 10354688 | tf_op jit(solution)/shard_map/dot_general | solution.py:29
  140.2 0.0 copy-start.1
  140.2 0.0 copy-start.7
  140.2 2.5 fusion.8
  142.8 299.8 %reduce-scatter.2.cloned.1.call-done = f32[64,1024]{1,0:T(8,128)} async-done(((f32[4096,1024]{1,0:T(8,128)}), f32[64,1024]{1,0:T(8,128)}) %reduce-scatter.2.cloned.1.call-update) | async-done | bytes 262160 | tf_op jit(solution)/shard_map/reduce_scatter | solution.py:32
  442.5 1.0 bitcast_subtract_fusion
  443.6 0.0 copy-start.6
  443.6 0.7 copy-done.6
  (13 shorter events, 0.1 us)
Async XLA Ops:
  8.0 5.2 %copy-start = (bf16[1,192,4096]{2,1,0:T(8,128)(2,1)S(1)}, bf16[1,192,4096]{2,1,0:T(8,128)(2,1)}, u32[]{:S(2)}) copy-start(bf16[1,192,4096]{2,1,0:T(8,128)(2,1)} %param.7) | copy-start | bytes 4718596
  8.0 55.7 %all-reduce.2.cloned.1.call-start = ((), (), s32[]{:S(2)}) async-start(), calls=%async_computation.3 | async-start | bytes 262144 | tf_op jit(solution)/shard_map/psum | solution.py:46
  11.4 121.2 %all-gather.2.cloned.1.call-start = ((), (), s32[]{:S(2)}) async-start(), calls=%async_computation.1 | async-start | bytes 8519680 | tf_op jit(solution)/shard_map/all_gather | solution.py:27
  13.1 429.4 %reduce-scatter.2.cloned.1.call-start = ((), (), s32[]{:S(2)}) async-start(), calls=%async_computation.2 | async-start | bytes 17039360 | tf_op jit(solution)/shard_map/reduce_scatter | solution.py:32
  22.3 41.4 %copy-start.4 = (f32[64,1024]{1,0:T(8,128)S(1)}, f32[64,1024]{1,0:T(8,128)}, u32[]{:S(2)}) copy-start(f32[64,1024]{1,0:T(8,128)} %param.11) | copy-start | bytes 786436
  22.3 110.3 %copy-start.5 = (bf16[1,192,1024]{2,1,0:T(8,128)(2,1)S(1)}, bf16[1,192,1024]{2,1,0:T(8,128)(2,1)}, u32[]{:S(2)}) copy-start(bf16[1,192,1024]{2,1,0:T(8,128)(2,1)} %param.8) | copy-start | bytes 1179652
  64.6 75.6 %copy-start.2 = (f32[64,1024]{1,0:T(8,128)}, f32[64,1024]{1,0:T(8,128)S(1)}, u32[]{:S(2)}) copy-start(f32[64,1024]{1,0:T(8,128)S(1)} %get-tuple-element.6) | copy-start | bytes 786436
  64.6 75.5 %copy-start.3 = (f32[64,1024]{1,0:T(8,128)}, f32[64,1024]{1,0:T(8,128)S(1)}, u32[]{:S(2)}) copy-start(f32[64,1024]{1,0:T(8,128)S(1)} %get-tuple-element.5) | copy-start | bytes 786436
  132.6 7.6 %copy-start.8 = (bf16[4096,1024]{1,0:T(8,128)(2,1)S(1)}, bf16[4096,1024]{1,0:T(8,128)(2,1)}, u32[]{:S(2)}) copy-start(bf16[4096,1024]{1,0:T(8,128)(2,1)} %all-gather.2.cloned.1.call-done) | copy-start | bytes 25165828
  140.2 302.3 %copy-start.1 = (f32[1,64,1024]{2,1,0:T(8,128)S(1)}, f32[1,64,1024]{2,1,0:T(8,128)}, u32[]{:S(2)}) copy-start(f32[1,64,1024]{2,1,0:T(8,128)} %param.9) | copy-start | bytes 786436
  140.2 303.3 %copy-start.7 = (f32[64,512]{1,0:T(8,128)S(1)}, f32[64,512]{1,0:T(8,128)}, u32[]{:S(2)}) copy-start(f32[64,512]{1,0:T(8,128)} %param.12) | copy-start | bytes 393220
  443.6 0.7 copy-start.6
Sparse Core Ops, SparseCore 0:
  12.0 51.5 all-reduce.1
Sparse Core Ops, SparseCore 1:
  14.3 118.3 all-gather.1
  135.0 307.4 reduce-scatter.1
where the time goes:
time: 456 us; the launch traced here: 452 us
  waiting for transfers between devices  409 us (90%)
  matrix products  19.2 us (4%)
  between operations  16.2 us (4%)
  other arithmetic  5.17 us (1%)
    reduce_scatter x1, waiting for transfers between devices, local(): lax.psum_scatter(lax.dot_general(rows, cotangent, contract_rows, preferre...  300 us
    all_gather x1, waiting for transfers between devices, local(): full_weight = lax.all_gather(weight_bf, 'fsdp', axis=0, tiled=True)  68 us
    psum x1, waiting for transfers between devices, local(): delta_sum = lax.psum(delta, 'rep')  41.4 us
  transfers between devices with their start and end apart: 3, of which 3 were waited for; matrix products, arithmetic and copies ran while one was open for 5% of the time, Pallas kernels for 0%

commit v1 on v0

v1 whole, which is shorter than its diff:
```python
import jax
import jax.numpy as jnp
from jax import lax
from jax.experimental import pallas as pl
from jax.experimental.pallas import tpu as pltpu
from jax.sharding import PartitionSpec as P

inner_rate = 0.0001
outer_rate = 0.7
moment_keep = 0.9
merge_keep = 0.5

MESH = pl.DeviceIdType.MESH
F32, BF16, I16, I32 = jnp.float32, jnp.bfloat16, jnp.int16, jnp.int32
T = 192
D = 4096
KW = 512
H = 256
TOP = 32766.0


def exponent_for(bound):
    return jnp.ceil(8.0 * jnp.log2(jnp.maximum(bound, 1e-30) * (1.0 / TOP)))


def step_of(exponent):
    return jnp.exp2(exponent * 0.125)


def encode(values, inverse):
    return jnp.round(values * inverse).astype(I32).astype(I16)


def decode(codes, step):
    return codes.astype(I32).astype(F32) * step


def kernel(
    fragment, x_hbm, g_hbm, lw_hbm, gw_hbm, om_hbm, ar_hbm,
    kv_hbm, gi_hbm, ln_hbm, gn_hbm, mn_hbm,
    xo, xs, go, gs, gt, lw, gw, om, ar, wa, wb, pt, top,
    a1s, a1r, a2s, a2r, a3s, a3r, acc, kva, gia, kvo, gio,
    gr, gx, dl, dr, lno, gno, mno,
    lsem, ssem, rsem,
):
    r = lax.axis_index("rep")
    f = lax.axis_index("fsdp")
    z, y, x, c = f // 32, (f // 8) % 4, (f // 2) % 4, f % 2

    def dev(z_, y_, x_, c_):
        return (r, ((z_ * 4 + y_) * 4 + x_) * 2 + c_)

    sib = dev(z, y, x, 1 - c)
    ring_id = ((lambda d: dev(z, y, (x + d) % 4, c)), (lambda d: dev(z, (y + d) % 4, x, c)))
    flip = (z, 1 - z)
    direct_id = (
        (lambda dz, d: dev(flip[dz], (y + d) % 4, x, c)),
        (lambda dz, d: dev(flip[dz], y, (x + d) % 4, c)),
    )
    offsets = [(dz, d) for dz in range(2) for d in range(4) if (dz, d) != (0, 0)]
    p = (x, y)
    o = (z * 4 + y, z * 4 + x)
    w = (wa, wb)
    cols = (slice(0, 512), slice(512, 1024))

    def other(g, dz, d):
        return flip[dz] * 4 + ((y, x)[g] + d) % 4

    def chunk(g, o_, p_):
        if g == 0:
            return o_ * 4 + p_
        return (o_ // 4) * 16 + p_ * 4 + o_ % 4

    counts = [0, 0]
    sends = []

    def remote(src, dst, to):
        i = counts[0]
        counts[0] += 1
        cp = pltpu.make_async_remote_copy(
            src_ref=src, dst_ref=dst, send_sem=ssem.at[i], recv_sem=rsem.at[i], device_id=to, device_id_type=MESH
        )
        cp.start()
        sends.append(cp)
        return cp

    def local(src, dst):
        i = counts[1]
        counts[1] += 1
        cp = pltpu.make_async_copy(src, dst, lsem.at[i])
        cp.start()
        return cp

    partners = [sib]
    partners += [direct_id[0](dz, d) for dz, d in offsets]
    partners += [direct_id[1](dz, d) for dz, d in offsets if d != 0]
    partners += [((r + d) % 4, f) for d in (1, 2, 3)]
    barrier = pltpu.get_barrier_semaphore()
    for to in partners:
        pl.semaphore_signal(barrier, inc=1, device_id=to, device_id_type=MESH)

    lw_in = local(lw_hbm.at[0], lw)
    go_in = local(g_hbm.at[0], go)
    Q = D // 4
    xo_in = [local(x_hbm.at[0, :, pl.ds(Q * i, Q)], xo.at[:, pl.ds(Q * i, Q)]) for i in range(4)]
    gw_in = local(gw_hbm, gw)
    om_in = local(om_hbm, om)
    ar_in = local(ar_hbm, ar)

    lw_in.wait()
    wa[x, c, o[0]] = lw[:, 0:512].astype(BF16)
    wb[y, c, o[1]] = lw[:, 512:1024].astype(BF16)
    gw_in.wait()
    first = fragment[0] % 2 == 0
    gsel = jnp.where(first, gw[:, 0:KW], gw[:, KW:])
    dl[...] = gsel - jnp.where(first, lw[:, 0:KW], lw[:, KW:])

    pl.semaphore_wait(barrier, len(partners))

    ag1 = [
        [remote(w[g].at[p[g], c, o[g]], w[g].at[p[g], c, o[g]], direct_id[g](dz, d)) for dz, d in offsets]
        for g in range(2)
    ]
    sib_cols = pl.ds(pl.multiple_of((1 - c) * KW, KW), KW)
    my_cols = pl.ds(pl.multiple_of(c * KW, KW), KW)
    gs_in = remote(g_hbm.at[0, :, sib_cols], gs, sib)
    xs_in = [remote(x_hbm.at[0, :, pl.ds(Q * i, Q)], xs.at[:, pl.ds(Q * i, Q)], sib) for i in range(4)]
    rep_in = [remote(dl, dr.at[d - 1], ((r + d) % 4, f)) for d in (1, 2, 3)]

    go_in.wait()
    gt[:, 0:T] = go[:, my_cols].T
    gs_in.wait_recv()
    gt[:, T:] = gs[...].T
    kva[...] = jnp.zeros_like(kva)
    gia[...] = jnp.zeros_like(gia)
    top[...] = jnp.zeros_like(top)

    ag2 = []
    agd = [{}, {}]
    for g in range(2):
        for cp in ag1[g]:
            cp.wait_recv()
        mine = w[g].at[p[g], c]
        ag2.append([remote(mine, mine, ring_id[g](1)), remote(mine, mine, ring_id[g](3))])
        agd[g][0] = [remote(mine, mine, sib)]

    for i in range(4):
        xo_in[i].wait()
        xs_in[i].wait_recv()

        def block(n, carry):
            lanes = pl.ds(pl.multiple_of(Q * i + n * 256, 256), 256)
            rows = jnp.concatenate([xo[:, lanes], xs[:, lanes]], axis=0)
            part = jnp.dot(gt[...], rows, preferred_element_type=F32)
            pt[8 * i + 2 * n] = part[:, 0:128]
            pt[8 * i + 2 * n + 1] = part[:, 128:256]
            size = jnp.max(jnp.abs(part).reshape(64, 8, 256), axis=0)
            top[...] = jnp.maximum(top[...], jnp.maximum(size[:, 0:128], size[:, 128:256]))
            return carry

        lax.fori_loop(0, 4, block, 0)

    bound0 = jnp.broadcast_to(jnp.max(top[...], axis=(0, 1), keepdims=True), (8, 128))
    e0 = exponent_for(bound0)
    inv0 = step_of(-e0)[0:1]

    def tag(exponent):
        e16 = exponent.astype(I32).astype(I16)
        return jnp.concatenate([e16, e16], axis=0)

    def tag_of(ref_rows):
        e = ref_rows[...].astype(I32).astype(F32)[0:8]
        return e, step_of(e)

    base = (0, H)
    rs1 = []
    for g in range(2):
        pair = []
        for s in range(2):
            buf = a1s.at[g, s]

            def enc1(k, carry, g=g, s=s, buf=buf):
                part = pt[chunk(g, k, (p[g] + 2) % 4), pl.ds(base[g] + 128 * s, 128)]
                buf[pl.ds(pl.multiple_of(k * 128, 128), 128)] = encode(part, inv0)
                return carry

            lax.fori_loop(0, 8, enc1, 0)
            buf[pl.ds(1024, 16)] = tag(e0)
            pair.append(remote(buf, a1r.at[g, s], ring_id[g]((1, 3)[s])))
        rs1.append(pair)

    rs2 = []
    bound2 = []
    for g in range(2):
        pair = []
        for s in range(2):
            rs1[g][s].wait_recv()
            got = a1r.at[g, s]
            buf = a2s.at[g, s]
            _, step1 = tag_of(got.at[pl.ds(1024, 16)])
            e2 = exponent_for(bound0 + step1 * TOP)
            inv2 = step_of(-e2)[0:1]
            step1 = step1[0:1]

            def enc2(k, carry, g=g, s=s, buf=buf, got=got, inv2=inv2, step1=step1):
                at = chunk(g, k, (p[g] + (1, 3)[s]) % 4)
                fed = pt[at, pl.ds(base[g] + 128 * s, 128)] + decode(
                    got[pl.ds(pl.multiple_of(k * 128, 128), 128)], step1
                )
                plain = pt[at, pl.ds(base[g] + 128 * (1 - s), 128)]
                buf[pl.ds(pl.multiple_of(k * 256 + 128 * s, 128), 128)] = encode(fed, inv2)
                buf[pl.ds(pl.multiple_of(k * 256 + 128 * (1 - s), 128), 128)] = encode(plain, inv2)
                return carry

            lax.fori_loop(0, 8, enc2, 0)
            buf[pl.ds(2048, 16)] = tag(e2)
            pair.append(remote(buf, a2r.at[g, s], ring_id[g]((1, 3)[s])))
        rs2.append(pair)

    def multiply(g, place, lo, hi):
        def pairs(k, carry):
            parts = []
            lanes = []
            for j in range(2):
                parts += [w[g][place, 0, 2 * k + j], w[g][place, 1, 2 * k + j]]
                lanes.append(pl.ds(pl.multiple_of(chunk(g, 2 * k + j, place) * 128, 128), 128))
            tile = jnp.concatenate(parts, axis=0)
            rows = jnp.concatenate([xo[:, lanes[0]], xo[:, lanes[1]]], axis=1)
            kva[:, cols[g]] += jnp.dot(rows, tile, preferred_element_type=F32)
            back = lax.dot_general(go[:, cols[g]], tile, (((1,), (1,)), ((), ())), preferred_element_type=F32)
            gia[:, lanes[0]] += back[:, 0:128]
            gia[:, lanes[1]] += back[:, 128:256]
            return carry

        lax.fori_loop(lo, hi, pairs, 0)

    ag3 = []
    for g in range(2):
        pair = []
        for s in range(2):
            ag2[g][s].wait_recv()
            src = (p[g] + (3, 1)[s]) % 4
            half = w[g].at[src, c, pl.ds(4 * s, 4)]
            pair.append(remote(half, half, ring_id[g]((1, 3)[s])))
            whole = w[g].at[src, c]
            agd[g][1 + s] = [remote(whole, whole, sib)]
        ag3.append(pair)

    for g in range(2):
        agd[g][0][0].wait_recv()
        multiply(g, p[g], 0, 4)

    for cp in rep_in:
        cp.wait_recv()
    om_in.wait()
    mean_delta = (dl[...] + dr[0] + dr[1] + dr[2]) * 0.25
    moment_new = moment_keep * jnp.where(first, om[:, 0:KW], om[:, KW:]) + mean_delta
    global_new = gsel - outer_rate * (mean_delta + moment_keep * moment_new)
    for h in range(2):
        sel = first if h == 0 else jnp.logical_not(first)
        mno[:, KW * h : KW * (h + 1)] = jnp.where(sel, moment_new, om[:, KW * h : KW * (h + 1)])
        gno[:, KW * h : KW * (h + 1)] = jnp.where(sel, global_new, gw[:, KW * h : KW * (h + 1)])
    outs = [local(mno, mn_hbm), local(gno, gn_hbm)]

    rs3 = []
    for g in range(2):
        steps = []
        total = bound0
        for s in range(2):
            rs2[g][s].wait_recv()
            _, st = tag_of(a2r.at[g, s, pl.ds(2048, 16)])
            steps.append(st[0:1])
            total = total + st * TOP
        e3 = exponent_for(total)
        inv3 = step_of(-e3)[0:1]
        tag3 = tag(e3)

        def summed(k, g=g, steps=steps):
            rows = pl.ds(pl.multiple_of(k * 256, 256), 256)
            return (
                pt[chunk(g, k, p[g]), pl.ds(base[g], H)]
                + decode(a2r[g, 0, rows], steps[0])
                + decode(a2r[g, 1, rows], steps[1])
            )

        group = []
        for j, (dz, d) in enumerate(offsets):
            a3s[g, j, 0:H] = encode(summed(other(g, dz, d)), inv3)
            a3s[g, j, H:] = tag3
            group.append(remote(a3s.at[g, j], a3r.at[g, j], direct_id[g](dz, d)))
        acc[pl.ds(base[g], H)] = summed(o[g])
        rs3.append(group)

    for g in range(2):
        for s in range(2):
            agd[g][1 + s][0].wait_recv()
            multiply(g, (p[g] + (3, 1)[s]) % 4, 0, 4)

    far = []
    for g in range(2):
        for s in range(2):
            ag3[g][s].wait_recv()
            half = w[g].at[(p[g] + 2) % 4, c, pl.ds(4 * s, 4)]
            far.append(remote(half, half, sib))

    for g in range(2):
        for j, cp in enumerate(rs3[g]):
            cp.wait_recv()
            _, st = tag_of(a3r.at[g, j, pl.ds(H, 16)])
            acc[pl.ds(base[g], H)] += decode(a3r[g, j, 0:H], st[0:1])
    gr[...] = acc[...].T
    gx_in = remote(gr.at[pl.ds(pl.multiple_of((1 - c) * 64, 64), 64)], gx, sib)

    for g in range(2):
        for s in range(2):
            far[2 * g + s].wait_recv()
            multiply(g, (p[g] + 2) % 4, 2 * s, 2 * s + 2)

    kvo[...] = kva[...].astype(BF16)
    gio[...] = gia[...].astype(BF16)
    outs += [local(kvo, kv_hbm.at[0]), local(gio, gi_hbm.at[0])]

    ar_in.wait()
    gx_in.wait_recv()

    def finish(gradient, at, is_first):
        inner = lw[:, at] - inner_rate * gradient
        sel = first if is_first else jnp.logical_not(first)
        merged = merge_keep * inner + (1.0 - merge_keep) * ar[...]
        lno[:, at] = jnp.where(sel, merged, inner)

    here = gr[pl.ds(pl.multiple_of(c * 64, 64), 64)]
    there = gx[...]
    finish(jnp.where(c == 0, here, there), slice(0, KW), True)
    finish(jnp.where(c == 0, there, here), slice(KW, 2 * KW), False)
    outs.append(local(lno, ln_hbm.at[0]))

    for cp in sends:
        cp.wait_send()
    for cp in outs:
        cp.wait()


N_REMOTE = 80
N_LOCAL = 16


def device_step(inputs, grad_kv, local_weight, global_weight, outer_moment, arrived, fragment):
    hbm = pl.BlockSpec(memory_space=pl.ANY)
    R = D // 64
    V = pltpu.VMEM
    return pl.pallas_call(
        kernel,
        out_shape=(
            jax.ShapeDtypeStruct((1, T, 2 * KW), BF16),
            jax.ShapeDtypeStruct((1, T, D), BF16),
            jax.ShapeDtypeStruct((1, R, 2 * KW), F32),
            jax.ShapeDtypeStruct((R, 2 * KW), F32),
            jax.ShapeDtypeStruct((R, 2 * KW), F32),
        ),
        in_specs=[pl.BlockSpec(memory_space=pltpu.SMEM)] + [hbm] * 6,
        out_specs=[hbm] * 5,
        scratch_shapes=[
            V((T, D), BF16), V((T, D), BF16),
            V((T, 2 * KW), BF16), V((T, KW), BF16), V((KW, 2 * T), BF16),
            V((R, 2 * KW), F32), V((R, 2 * KW), F32), V((R, 2 * KW), F32), V((R, KW), F32),
            V((4, 2, 8, R, KW), BF16), V((4, 2, 8, R, KW), BF16),
            V((32, KW, 128), F32), V((8, 128), F32),
            V((2, 2, 1040, 128), I16), V((2, 2, 1040, 128), I16),
            V((2, 2, 2064, 128), I16), V((2, 2, 2064, 128), I16),
            V((2, 7, H + 16, 128), I16), V((2, 7, H + 16, 128), I16),
            V((KW, 128), F32), V((T, 2 * KW), F32), V((T, D), F32),
            V((T, 2 * KW), BF16), V((T, D), BF16),
            V((128, KW), F32), V((R, KW), F32), V((R, KW), F32), V((3, R, KW), F32),
            V((R, 2 * KW), F32), V((R, 2 * KW), F32), V((R, 2 * KW), F32),
            pltpu.SemaphoreType.DMA((N_LOCAL,)),
            pltpu.SemaphoreType.DMA((N_REMOTE,)),
            pltpu.SemaphoreType.DMA((N_REMOTE,)),
        ],
        compiler_params=pltpu.CompilerParams(
            collective_id=0, has_side_effects=True, vmem_limit_bytes=60 * 1024 * 1024
        ),
        name="step",
    )(fragment, inputs, grad_kv, local_weight, global_weight, outer_moment, arrived)


def solution(mesh):
    return jax.shard_map(
        device_step,
        mesh=mesh,
        in_specs=(
            P("rep", "fsdp", None),
            P("rep", "fsdp", None),
            P("rep", "fsdp", None),
            P("fsdp", None),
            P("fsdp", None),
            P("fsdp", None),
            P(),
        ),
        out_specs=(
            P("rep", "fsdp", None),
            P("rep", "fsdp", None),
            P("rep", "fsdp", None),
            P("fsdp", None),
            P("fsdp", None),
        ),
        check_vma=False,
    )
```

time: 456 us -> 82.5 us (0.18)
  waiting for transfers between devices: 409 us -> 0 us
  Pallas kernels: 0 us -> 74 us
  matrix products: 19.2 us -> 0 us
  between operations: 16.2 us -> 1.29 us
  other arithmetic: 5.17 us -> 0 us
  local copies, waits for them, and re-layouts: 1.82 us -> 6.66 us
    reduce_scatter x1 -> x0, waiting for transfers between devices: 300 us -> none  [local(): lax.psum_scatter(lax.dot_general(rows, cotangent, contract_rows, preferre...]
    pallas_call x0 -> x1, Pallas kernels: none -> 74 us  [device_step(): pl.pallas_call(kernel, out_shape=(jax.ShapeDtypeStruct((1, T, 2 * KW), BF...]
    all_gather x1 -> x0, waiting for transfers between devices: 68 us -> none  [local(): full_weight = lax.all_gather(weight_bf, 'fsdp', axis=0, tiled=True)]
    psum x1 -> x0, waiting for transfers between devices: 41.4 us -> none  [local(): delta_sum = lax.psum(delta, 'rep')]
    dot_general x3 -> x0, matrix products: 19.2 us -> none  [the longest x1 9.11 us: local(): lax.dot_general(rows, cotangent, contract_rows, preferred_element_type=jn...]
    unnamed x20 -> x11, local copies, waits for them, and re-layouts: 1.82 us -> 6.66 us
  transfers between devices with their start and end apart: 3 -> 0, of which waited for: 3 -> 0; matrix products, arithmetic and copies ran while one was open for 5% -> 0% of each run, Pallas kernels for 0% -> 0%
where the time goes in v1:
time: 82.5 us; the launch traced here: 81.9 us
  Pallas kernels  74 us (90%)
  local copies, waits for them, and re-layouts  6.66 us (8%)
  between operations  1.29 us (2%)
    pallas_call x1, Pallas kernels, device_step(): pl.pallas_call(kernel, out_shape=(jax.ShapeDtypeStruct((1, T, 2 * KW), BF...  74 us
    unnamed x11, local copies, waits for them, and re-layouts  6.66 us

profile of v1, /device:TPU:1, one launch (start us, length us, event | category | flops | bytes accessed | tf_op | source)
XLA Modules:
  0.0 81.9 jit_solution(6662337680609429816)
XLA Ops:
  1.3 74.0 %step.1 = (bf16[1,192,1024]{2,1,0:T(8,128)(2,1)}, bf16[1,192,4096]{2,1,0:T(8,128)(2,1)}, f32[1,64,1024]{2,1,0:T(8,128)}, f32[64,1024]{1,0:T(8,128)}, f32[64,1024]{1,0:T(8,128)}) custom-call(s32[1]{0:T(128)S(6)} %copy.17.fragment, bf16[1,192,4096]{2,1,0:T(8,128)(2,1)} %x_hbm.1, bf16[1,192,1024]{2,1,0:T(8,128)(2,1)} %g_hbm.1, f32[1,64,1024]{2,1,0:T(8,128)} %lw_hbm.1, ...), custom_call_target="tpu_custom_call" | custom-call | tf_op jit(solution)/shard_map/step/pallas_call | solution.py:352
  75.3 1.8 %copy.18 = bf16[1,192,1024]{2,1,0:T(8,128)(2,1)} copy(bf16[1,192,1024]{2,1,0:T(8,128)(2,1)} %get-tuple-element.10) | data formatting | bytes 786432
  77.0 0.0 copy-start.2
  77.1 0.0 copy-start.1
  77.1 0.0 copy-start
  77.1 2.8 %copy.19 = bf16[1,192,4096]{2,1,0:T(8,128)(2,1)} copy(bf16[1,192,4096]{2,1,0:T(8,128)(2,1)} %get-tuple-element.11) | data formatting | bytes 3145728
  79.8 0.0 copy-done.2
  79.8 0.7 copy.20
  80.5 0.0 copy-done.1
  80.5 0.7 copy.21
  81.2 0.0 copy-done
  81.2 0.7 copy.22
Async XLA Ops:
  77.0 2.8 %copy-start.2 = (f32[1,64,1024]{2,1,0:T(8,128)S(1)}, f32[1,64,1024]{2,1,0:T(8,128)}, u32[]{:S(2)}) copy-start(f32[1,64,1024]{2,1,0:T(8,128)} %get-tuple-element.12) | copy-start | bytes 786436
  77.1 3.5 %copy-start.1 = (f32[64,1024]{1,0:T(8,128)S(1)}, f32[64,1024]{1,0:T(8,128)}, u32[]{:S(2)}) copy-start(f32[64,1024]{1,0:T(8,128)} %get-tuple-element.13) | copy-start | bytes 786436
  77.1 4.2 %copy-start = (f32[64,1024]{1,0:T(8,128)S(1)}, f32[64,1024]{1,0:T(8,128)}, u32[]{:S(2)}) copy-start(f32[64,1024]{1,0:T(8,128)} %get-tuple-element.14) | copy-start | bytes 786436

commit v2 on v1

v2 whole, which is shorter than its diff:
```python
import jax
import jax.numpy as jnp
from jax import lax
from jax.experimental import pallas as pl
from jax.experimental.pallas import tpu as pltpu
from jax.sharding import PartitionSpec as P

inner_rate = 0.0001
outer_rate = 0.7
moment_keep = 0.9
merge_keep = 0.5

MESH = pl.DeviceIdType.MESH
F32, BF16, I16, I32 = jnp.float32, jnp.bfloat16, jnp.int16, jnp.int32
T = 192
D = 4096
KW = 512
H = 256
TOP = 32766.0


def exponent_for(bound):
    return jnp.ceil(8.0 * jnp.log2(jnp.maximum(bound, 1e-30) * (1.0 / TOP)))


def step_of(exponent):
    return jnp.exp2(exponent * 0.125)


def encode(values, inverse):
    return jnp.round(values * inverse).astype(I32).astype(I16)


def decode(codes, step):
    return codes.astype(I32).astype(F32) * step


def kernel(
    fragment_hbm, x_hbm, g_hbm, lw_hbm, gw_hbm, om_hbm, ar_hbm,
    kvo, gio, lno, gno, mno,
    xo, xs, go, gs, gt, lw, gw, om, ar, wa, wb, pt, top,
    c1s, c1r, a1os, a1or, a1xs, a1xr, a2os, a2or, a2xs, a2xr, a3s, a3r, a4s, a4r,
    acc, kva, gia,
    gr, gx, dl, ds, dr, fragment,
    lsem, ssem, rsem,
):
    r = lax.axis_index("rep")
    f = lax.axis_index("fsdp")
    z, y, x, c = f // 32, (f // 8) % 4, (f // 2) % 4, f % 2
    zx = 1 - z

    def dev(z_, y_, x_, c_):
        return (r, ((z_ * 4 + y_) * 4 + x_) * 2 + c_)

    sib = dev(z, y, x, 1 - c)
    zid = dev(zx, y, x, c)
    ids = ((lambda d: dev(z, y, (x + d) % 4, c)), (lambda d: dev(z, (y + d) % 4, x, c)))
    ring_id = ids
    line_id = (ids[1], ids[0])
    p = (x, y)
    q = (y, x)
    w = (wa, wb)
    cols = (slice(0, KW), slice(KW, 2 * KW))
    base = (0, H)
    own, oth = pl.ds(4 * z, 4), pl.ds(4 * zx, 4)
    turn = (1, 3)

    def chunk(g, plane, q_, p_):
        return plane * 16 + (q_ * 4 + p_ if g == 0 else p_ * 4 + q_)

    counts = [0, 0]
    sends = []

    def remote(src, dst, to):
        i = counts[0]
        counts[0] += 1
        cp = pltpu.make_async_remote_copy(
            src_ref=src, dst_ref=dst, send_sem=ssem.at[i], recv_sem=rsem.at[i], device_id=to, device_id_type=MESH
        )
        cp.start()
        sends.append(cp)
        return cp

    def same(ref, to):
        return remote(ref, ref, to)

    def local(src, dst):
        i = counts[1]
        counts[1] += 1
        cp = pltpu.make_async_copy(src, dst, lsem.at[i])
        cp.start()
        return cp

    partners = [sib, zid]
    partners += [ids[0](d) for d in (1, 2, 3)] + [ids[1](d) for d in (1, 2, 3)]
    partners += [((r + d) % 4, f) for d in (1, 2, 3)]
    barrier = pltpu.get_barrier_semaphore()
    for to in partners:
        pl.semaphore_signal(barrier, inc=1, device_id=to, device_id_type=MESH)

    lw_in = local(lw_hbm.at[0], lw)
    fragment_in = local(fragment_hbm, fragment)
    go_in = local(g_hbm.at[0], go)
    Q = D // 4
    xo_in = [local(x_hbm.at[0, :, pl.ds(Q * i, Q)], xo.at[:, pl.ds(Q * i, Q)]) for i in range(4)]
    gw_in = local(gw_hbm, gw)
    om_in = local(om_hbm, om)
    ar_in = local(ar_hbm, ar)

    lw_in.wait()
    for g in range(2):
        w[g][p[g], c, 4 * z + q[g]] = lw[:, cols[g]].astype(BF16)

    pl.semaphore_wait(barrier, len(partners))

    N = 3 * KW // 4
    ag0 = [same(w[g].at[p[g], c, 4 * z + q[g], :, 0:N], zid) for g in range(2)]
    ag1 = [[same(w[g].at[p[g], c, 4 * z + q[g]], line_id[g](d)) for d in (1, 2, 3)] for g in range(2)]
    sib_cols = pl.ds(pl.multiple_of((1 - c) * KW, KW), KW)
    my_cols = pl.ds(pl.multiple_of(c * KW, KW), KW)
    gs_in = remote(g_hbm.at[0, :, sib_cols], gs, sib)
    xs_in = [remote(x_hbm.at[0, :, pl.ds(Q * i, Q)], xs.at[:, pl.ds(Q * i, Q)], sib) for i in range(4)]

    def tag(exponent):
        e16 = exponent.astype(I32).astype(I16)
        return jnp.concatenate([e16, e16], axis=0)

    def tag_of(rows):
        e = rows.astype(I32).astype(F32)[0:8]
        return step_of(e)

    def largest(values):
        return jnp.broadcast_to(jnp.max(values, axis=(0, 1), keepdims=True), (8, 128))

    gw_in.wait()
    fragment_in.wait()
    first = fragment[0] % 2 == 0
    gsel = jnp.where(first, gw[:, 0:KW], gw[:, KW:])
    dl[...] = gsel - jnp.where(first, lw[:, 0:KW], lw[:, KW:])
    ed = exponent_for(largest(jnp.abs(dl[...])))
    ds[0:64] = encode(dl[...], jnp.concatenate([step_of(-ed)[0:1]] * 4, axis=1))
    ds[64:80] = jnp.concatenate([tag(ed)] * 4, axis=1)

    go_in.wait()
    gt[:, 0:T] = go[:, my_cols].T
    gs_in.wait_recv()
    gt[:, T:] = gs[...].T
    kva[...] = jnp.zeros_like(kva)
    gia[...] = jnp.zeros_like(gia)
    top[...] = jnp.zeros_like(top)

    ag1x = []
    for g in range(2):
        ag0[g].wait_recv()
        ag1x.append([same(w[g].at[p[g], c, 4 * zx + q[g], :, 0:N], line_id[g](d)) for d in (1, 2, 3)])

    def cross(g, place):
        return same(w[g].at[place, c, own, :, N:KW], zid)

    def share(g, place, plane):
        return same(w[g].at[place, c, plane], sib)

    ag2, ag2x, ag3, ag3x = [], [], [], []
    cz = [{}, {}]
    so = [{}, {}]
    sx = [{}, {}]
    for g in range(2):
        for cp in ag1[g]:
            cp.wait_recv()
        mine = w[g].at[p[g], c, own]
        ag2.append([same(mine, ring_id[g](turn[s])) for s in range(2)])
        cz[g][0] = cross(g, p[g])
        so[g][0] = share(g, p[g], own)

    for i in range(4):
        xo_in[i].wait()
        xs_in[i].wait_recv()

        def block(n, carry):
            lanes = pl.ds(pl.multiple_of(Q * i + n * 256, 256), 256)
            rows = jnp.concatenate([xo[:, lanes], xs[:, lanes]], axis=0)
            part = jnp.dot(gt[...], rows, preferred_element_type=F32)
            pt[8 * i + 2 * n] = part[:, 0:128]
            pt[8 * i + 2 * n + 1] = part[:, 128:256]
            size = jnp.max(jnp.abs(part).reshape(64, 8, 256), axis=0)
            top[...] = jnp.maximum(top[...], jnp.maximum(size[:, 0:128], size[:, 128:256]))
            return carry

        lax.fori_loop(0, 4, block, 0)

    bound0 = largest(top[...])
    e0 = exponent_for(bound0)
    inv0 = step_of(-e0)[0:1]
    tag0 = tag(e0)

    stages = (2, 1, 3, 0)
    c1 = []
    for i, d in enumerate(stages):
        for g in range(2):

            def enc(k, carry, g=g, i=i, d=d):
                part = pt[chunk(g, zx, k, (p[g] + d) % 4), pl.ds(base[g] + 192, 64)]
                c1s[i, pl.ds(pl.multiple_of(256 * g + 64 * k, 64), 64)] = encode(part, inv0)
                return carry

            lax.fori_loop(0, 4, enc, 0)
        c1s[i, 512:528] = tag0
        c1.append(remote(c1s.at[i], c1r.at[i], zid))

    def crossed(i):
        c1[i].wait_recv()
        step = tag_of(c1r[i, 512:528])
        for g in range(2):

            def add(k, carry, g=g):
                at = chunk(g, z, k, (p[g] + stages[i]) % 4)
                rows = pl.ds(pl.multiple_of(256 * g + 64 * k, 64), 64)
                pt[at, pl.ds(base[g] + 192, 64)] += decode(c1r[i, rows], step[0:1])
                return carry

            lax.fori_loop(0, 4, add, 0)
        return step * TOP

    def hop1(g, s, plane, half, buf, dst, inv, mark):
        def enc(k, carry):
            part = pt[chunk(g, plane, k, (p[g] + 2) % 4), pl.ds(base[g] + half * s, half)]
            buf[pl.ds(pl.multiple_of(k * half, half), half)] = encode(part, inv)
            return carry

        lax.fori_loop(0, 4, enc, 0)
        buf[4 * half : 4 * half + 16] = mark
        return remote(buf, dst, ring_id[g](turn[s]))

    rs1x = [[hop1(g, s, zx, 96, a1xs.at[g, s], a1xr.at[g, s], inv0, tag0) for s in range(2)] for g in range(2)]

    for g in range(2):
        for cp in ag1x[g]:
            cp.wait_recv()
        ag2x.append([same(w[g].at[p[g], c, oth, :, 0:N], ring_id[g](turn[s])) for s in range(2)])
        cz[g][0].wait_recv()
        sx[g][0] = share(g, p[g], oth)

    bound_own = bound0 + crossed(0)
    e_own = exponent_for(bound_own)
    inv_own = step_of(-e_own)[0:1]
    tag_own = tag(e_own)
    rs1 = [[hop1(g, s, z, 128, a1os.at[g, s], a1or.at[g, s], inv_own, tag_own) for s in range(2)] for g in range(2)]

    rep_in = [remote(ds, dr.at[d - 1], ((r + d) % 4, f)) for d in (1, 2, 3)]

    def hop2(g, s, plane, half, copy, got, buf, dst, bound):
        copy.wait_recv()
        step = tag_of(got[4 * half : 4 * half + 16])
        e = exponent_for(bound + step * TOP)
        inv = step_of(-e)[0:1]
        step = step[0:1]

        def enc(k, carry):
            at = chunk(g, plane, k, (p[g] + turn[s]) % 4)
            fed = pt[at, pl.ds(base[g] + half * s, half)] + decode(got[pl.ds(pl.multiple_of(k * half, half), half)], step)
            plain = pt[at, pl.ds(base[g] + half * (1 - s), half)]
            buf[pl.ds(pl.multiple_of(2 * k * half + half * s, half), half)] = encode(fed, inv)
            buf[pl.ds(pl.multiple_of(2 * k * half + half * (1 - s), half), half)] = encode(plain, inv)
            return carry

        lax.fori_loop(0, 4, enc, 0)
        buf[8 * half : 8 * half + 16] = tag(e)
        return remote(buf, dst, ring_id[g](turn[s]))

    rs2x = [
        [
            hop2(g, s, zx, 96, rs1x[g][s], a1xr.at[g, s], a2xs.at[g, s], a2xr.at[g, s], bound0)
            for s in range(2)
        ]
        for g in range(2)
    ]

    for g in range(2):
        pair = []
        for s in range(2):
            ag2[g][s].wait_recv()
            src = (p[g] + turn[1 - s]) % 4
            pair.append(same(w[g].at[src, c, pl.ds(4 * z + 2 * s, 2)], ring_id[g](turn[s])))
            cz[g][1 + s] = cross(g, src)
            so[g][1 + s] = share(g, src, own)
        ag3.append(pair)

    crossed(1)
    crossed(2)
    rs2 = [
        [
            hop2(g, s, z, 128, rs1[g][s], a1or.at[g, s], a2os.at[g, s], a2or.at[g, s], bound_own)
            for s in range(2)
        ]
        for g in range(2)
    ]

    for g in range(2):
        pair = []
        for s in range(2):
            ag2x[g][s].wait_recv()
            src = (p[g] + turn[1 - s]) % 4
            pair.append(same(w[g].at[src, c, pl.ds(4 * zx + 2 * s, 2), :, 0:N], ring_id[g](turn[s])))
            cz[g][1 + s].wait_recv()
            sx[g][1 + s] = share(g, src, oth)
        ag3x.append(pair)

    def multiply(g, place, plane, copy):
        copy.wait_recv()
        parts = []
        rows = []
        lanes = []
        for k in range(4):
            parts += [w[g][place, 0, 4 * plane + k], w[g][place, 1, 4 * plane + k]]
            lanes.append(pl.ds(pl.multiple_of(chunk(g, plane, k, place) * 128, 128), 128))
            rows.append(xo[:, lanes[k]])
        tile = jnp.concatenate(parts, axis=0)
        kva[:, cols[g]] += jnp.dot(jnp.concatenate(rows, axis=1), tile, preferred_element_type=F32)
        back = lax.dot_general(go[:, cols[g]], tile, (((1,), (1,)), ((), ())), preferred_element_type=F32)
        for k in range(4):
            gia[:, lanes[k]] += back[:, 128 * k : 128 * (k + 1)]

    for g in range(2):
        multiply(g, p[g], z, so[g][0])
        multiply(g, p[g], zx, sx[g][0])

    crossed(3)
    rs3 = []
    bound_x = []
    for g in range(2):
        steps = []
        total, total_x = bound_own, bound0
        for s in range(2):
            rs2x[g][s].wait_recv()
            st_x = tag_of(a2xr[g, s, 768:784])
            rs2[g][s].wait_recv()
            st = tag_of(a2or[g, s, 1024:1040])
            steps.append((st[0:1], st_x[0:1]))
            total, total_x = total + st * TOP, total_x + st_x * TOP
        bound_x.append(total_x)
        e3 = exponent_for(jnp.maximum(total, total_x))
        inv3 = step_of(-e3)[0:1]
        tag3 = tag(e3)

        def sum_own(k, g=g, steps=steps):
            rows = pl.ds(pl.multiple_of(k * 256, 256), 256)
            return (
                pt[chunk(g, z, k, p[g]), pl.ds(base[g], 256)]
                + decode(a2or[g, 0, rows], steps[0][0])
                + decode(a2or[g, 1, rows], steps[1][0])
            )

        def sum_oth(k, g=g, steps=steps):
            rows = pl.ds(pl.multiple_of(k * 192, 192), 192)
            return (
                pt[chunk(g, zx, k, p[g]), pl.ds(base[g], 192)]
                + decode(a2xr[g, 0, rows], steps[0][1])
                + decode(a2xr[g, 1, rows], steps[1][1])
            )

        group = []
        for d in (1, 2, 3):
            a3s[g, d - 1, 0:256] = encode(sum_own((q[g] + d) % 4), inv3)
            a3s[g, d - 1, 256:448] = encode(sum_oth((q[g] + d) % 4), inv3)
            a3s[g, d - 1, 448:464] = tag3
            group.append(remote(a3s.at[g, d - 1], a3r.at[g, d - 1], line_id[g](d)))
        acc[pl.ds(base[g], 256)] = sum_own(q[g])
        pt[chunk(g, zx, q[g], p[g]), pl.ds(base[g], 192)] = sum_oth(q[g])
        rs3.append(group)

    for g in range(2):
        far = (p[g] + 2) % 4
        for s in range(2):
            ag3[g][s].wait_recv()
        cz[g][3] = cross(g, far)
        so[g][3] = share(g, far, own)

    rs4 = []
    for g in range(2):
        total = bound_x[g]
        steps = []
        for j in range(3):
            rs3[g][j].wait_recv()
            steps.append(tag_of(a3r[g, j, 448:464]))
            total = total + steps[j] * TOP
        e4 = exponent_for(total)
        part = pt[chunk(g, zx, q[g], p[g]), pl.ds(base[g], 192)]
        for j in range(3):
            part = part + decode(a3r[g, j, 256:448], steps[j][0:1])
        a4s[g, 0:192] = encode(part, step_of(-e4)[0:1])
        a4s[g, 192:208] = tag(e4)
        rs4.append(remote(a4s.at[g], a4r.at[g], zid))
        part = acc[pl.ds(base[g], 256)]
        for j in range(3):
            part = part + decode(a3r[g, j, 0:256], steps[j][0:1])
        acc[pl.ds(base[g], 256)] = part

    for g in range(2):
        for s in range(2):
            src = (p[g] + turn[1 - s]) % 4
            multiply(g, src, z, so[g][1 + s])
            multiply(g, src, zx, sx[g][1 + s])

    for g in range(2):
        rs4[g].wait_recv()
        step = tag_of(a4r[g, 192:208])
        acc[pl.ds(base[g], 192)] += decode(a4r[g, 0:192], step[0:1])
    gr[...] = acc[...].T
    gx_in = remote(gr.at[pl.ds(pl.multiple_of((1 - c) * 64, 64), 64)], gx, sib)

    for g in range(2):
        far = (p[g] + 2) % 4
        for s in range(2):
            ag3x[g][s].wait_recv()
        cz[g][3].wait_recv()
        sx[g][3] = share(g, far, oth)

    om_in.wait()
    mean_delta = dl[...]
    for j in range(3):
        rep_in[j].wait_recv()
        step = tag_of(dr[j, 64:80])
        mean_delta = mean_delta + decode(dr[j, 0:64], step[0:1])
    mean_delta = mean_delta * 0.25
    moment_new = moment_keep * jnp.where(first, om[:, 0:KW], om[:, KW:]) + mean_delta
    gsel = jnp.where(first, gw[:, 0:KW], gw[:, KW:])
    global_new = gsel - outer_rate * (mean_delta + moment_keep * moment_new)
    for h in range(2):
        sel = first if h == 0 else jnp.logical_not(first)
        mno[:, cols[h]] = jnp.where(sel, moment_new, om[:, cols[h]])
        gno[:, cols[h]] = jnp.where(sel, global_new, gw[:, cols[h]])

    for g in range(2):
        far = (p[g] + 2) % 4
        multiply(g, far, z, so[g][3])
    for g in range(2):
        far = (p[g] + 2) % 4
        multiply(g, far, zx, sx[g][3])

    kvo[...] = kva[...].astype(BF16)
    gio[...] = gia[...].astype(BF16)

    ar_in.wait()
    gx_in.wait_recv()

    def finish(gradient, at, is_first):
        inner = lw[:, at] - inner_rate * gradient
        sel = first if is_first else jnp.logical_not(first)
        merged = merge_keep * inner + (1.0 - merge_keep) * ar[...]
        lno[:, at] = jnp.where(sel, merged, inner)

    here = gr[pl.ds(pl.multiple_of(c * 64, 64), 64)]
    there = gx[...]
    finish(jnp.where(c == 0, here, there), slice(0, KW), True)
    finish(jnp.where(c == 0, there, here), slice(KW, 2 * KW), False)

    for cp in sends:
        cp.wait_send()
    assert counts[0] <= N_REMOTE and counts[1] <= N_LOCAL


def write_out(*refs):
    sem = refs[10]
    copies = [pltpu.make_async_copy(refs[i], refs[5 + i], sem.at[i]) for i in range(5)]
    for cp in copies:
        cp.start()
    for cp in copies:
        cp.wait()


N_REMOTE = 110
N_LOCAL = 16


def device_step(inputs, grad_kv, local_weight, global_weight, outer_moment, arrived, fragment):
    hbm = pl.BlockSpec(memory_space=pltpu.HBM)
    vmem = pl.BlockSpec(memory_space=pltpu.VMEM)
    R = D // 64
    V = pltpu.VMEM
    shapes = (((T, 2 * KW), BF16), ((T, D), BF16), ((R, 2 * KW), F32), ((R, 2 * KW), F32), ((R, 2 * KW), F32))
    held = pl.pallas_call(
        kernel,
        out_shape=tuple(V(shape, dtype) for shape, dtype in shapes),
        in_specs=[hbm] * 7,
        out_specs=[vmem] * 5,
        scratch_shapes=[
            V((T, D), BF16), V((T, D), BF16),
            V((T, 2 * KW), BF16), V((T, KW), BF16), V((KW, 2 * T), BF16),
            V((R, 2 * KW), F32), V((R, 2 * KW), F32), V((R, 2 * KW), F32), V((R, KW), F32),
            V((4, 2, 8, R, KW), BF16), V((4, 2, 8, R, KW), BF16),
            V((32, KW, 128), F32), V((8, 128), F32),
            V((4, 528, 128), I16), V((4, 528, 128), I16),
            V((2, 2, 528, 128), I16), V((2, 2, 528, 128), I16),
            V((2, 2, 400, 128), I16), V((2, 2, 400, 128), I16),
            V((2, 2, 1040, 128), I16), V((2, 2, 1040, 128), I16),
            V((2, 2, 784, 128), I16), V((2, 2, 784, 128), I16),
            V((2, 3, 464, 128), I16), V((2, 3, 464, 128), I16),
            V((2, 208, 128), I16), V((2, 208, 128), I16),
            V((KW, 128), F32), V((T, 2 * KW), F32), V((T, D), F32),
            V((128, KW), F32), V((R, KW), F32), V((R, KW), F32),
            V((R + 16, KW), I16), V((3, R + 16, KW), I16),
            pltpu.SMEM((1,), I32),
            pltpu.SemaphoreType.DMA((N_LOCAL,)),
            pltpu.SemaphoreType.DMA((N_REMOTE,)),
            pltpu.SemaphoreType.DMA((N_REMOTE,)),
        ],
        compiler_params=pltpu.CompilerParams(
            collective_id=0, has_side_effects=True, vmem_limit_bytes=60 * 1024 * 1024
        ),
        name="step",
    )(fragment, inputs, grad_kv, local_weight, global_weight, outer_moment, arrived)
    kv, gi, ln, gn, mn = pl.pallas_call(
        write_out,
        out_shape=tuple(jax.ShapeDtypeStruct(shape, dtype) for shape, dtype in shapes),
        in_specs=[vmem] * 5,
        out_specs=[hbm] * 5,
        scratch_shapes=[pltpu.SemaphoreType.DMA((5,))],
        compiler_params=pltpu.CompilerParams(vmem_limit_bytes=1024 * 1024),
        name="write",
    )(*(pltpu.with_memory_space_constraint(a, pltpu.VMEM) for a in held))
    return kv[None], gi[None], ln[None], gn, mn


def solution(mesh):
    return jax.shard_map(
        device_step,
        mesh=mesh,
        in_specs=(
            P("rep", "fsdp", None),
            P("rep", "fsdp", None),
            P("rep", "fsdp", None),
            P("fsdp", None),
            P("fsdp", None),
            P("fsdp", None),
            P(),
        ),
        out_specs=(
            P("rep", "fsdp", None),
            P("rep", "fsdp", None),
            P("rep", "fsdp", None),
            P("fsdp", None),
            P("fsdp", None),
        ),
        check_vma=False,
    )
```

time: 82.5 us -> 67 us (0.81)
  Pallas kernels: 74 us -> 65.6 us
  local copies, waits for them, and re-layouts: 6.66 us -> 0 us
    pallas_call x1 -> x2, Pallas kernels: 74 us -> 65.6 us  [the longest x1 64 us: device_step(): pl.pallas_call(kernel, out_shape=tuple((V(shape, dtype) for shape, dtype...]
    unnamed x11 -> x0, local copies, waits for them, and re-layouts: 6.66 us -> none
where the time goes in v2:
time: 67 us; the launch traced here: 66.9 us
  Pallas kernels  65.6 us (98%)
  between operations  1.29 us (2%)
    pallas_call x1, Pallas kernels, device_step(): pl.pallas_call(kernel, out_shape=tuple((V(shape, dtype) for shape, dtype...  64 us
    pallas_call x1, Pallas kernels, device_step(): pl.pallas_call(write_out, out_shape=tuple((jax.ShapeDtypeStruct(shape, dt...  1.57 us

profile of v2, /device:TPU:1, one launch (start us, length us, event | category | flops | bytes accessed | tf_op | source)
XLA Modules:
  0.0 66.9 jit_solution(14564647067517889442)
XLA Ops:
  1.3 64.0 %step.1 = (bf16[192,1024]{1,0:T(8,128)(2,1)S(1)}, bf16[192,4096]{1,0:T(8,128)(2,1)S(1)}, f32[64,1024]{1,0:T(8,128)S(1)}, f32[64,1024]{1,0:T(8,128)S(1)}, f32[64,1024]{1,0:T(8,128)S(1)}) custom-call(s32[1]{0:T(128)S(6)} %copy.12.fragment_hbm, bf16[1,192,4096]{2,1,0:T(8,128)(2,1)} %x_hbm.1, bf16[1,192,1024]{2,1,0:T(8,128)(2,1)} %g_hbm.1, ...), custom_call_target="tpu_custom_call" | custom-call | tf_op jit(solution)/shard_map/step/pallas_call | solution.py:481
  65.3 1.6 %write.1 = (bf16[192,1024]{1,0:T(8,128)(2,1)}, bf16[192,4096]{1,0:T(8,128)(2,1)}, f32[64,1024]{1,0:T(8,128)}, f32[64,1024]{1,0:T(8,128)}, f32[64,1024]{1,0:T(8,128)}) custom-call(bf16[192,1024]{1,0:T(8,128)(2,1)S(1)} %get-tuple-element.15.refs_0_, bf16[192,4096]{1,0:T(8,128)(2,1)S(1)} %get-tuple-element.16.refs_1_, ...), custom_call_target="tpu_custom_call" | custom-call | tf_op jit(solution)/shard_map/write/pallas_call | solution.py:512

commit v3 on v0

v3 whole, which is shorter than its diff:
```python
import jax
import jax.numpy as jnp
from jax import lax
from jax.experimental import pallas as pl
from jax.experimental.pallas import tpu as pltpu
from jax.sharding import PartitionSpec as P

inner_rate = 0.0001
outer_rate = 0.7
moment_keep = 0.9
merge_keep = 0.5

MESH = pl.DeviceIdType.MESH
F32, BF16, I16, I32 = jnp.float32, jnp.bfloat16, jnp.int16, jnp.int32
T = 192
D = 4096
KW = 512
H = 256
TOP = 32766.0


def exponent_for(bound):
    return jnp.ceil(8.0 * jnp.log2(jnp.maximum(bound, 1e-30) * (1.0 / TOP)))


def step_of(exponent):
    return jnp.exp2(exponent * 0.125)


def encode(values, inverse):
    return jnp.round(values * inverse).astype(I32).astype(I16)


def decode(codes, step):
    return codes.astype(I32).astype(F32) * step


def kernel(
    fragment_hbm, x_hbm, g_hbm, lw_hbm, gw_hbm, om_hbm, ar_hbm,
    kvo, gio, lno, gno, mno,
    xo, xs, go, gs, gt, lw, gw, om, ar, wa, wb, pt, top,
    c1s, c1r, a1os, a1or, a1xs, a1xr, a2os, a2or, a2xs, a2xr, a3os, a3or, a3xs, a3xr, a4s, a4r,
    acc, kva, gia,
    gr, gx, dl, ds, dr, fragment,
    lsem, ssem, rsem,
):
    r = lax.axis_index("rep")
    f = lax.axis_index("fsdp")
    z, y, x, c = f // 32, (f // 8) % 4, (f // 2) % 4, f % 2
    zx = 1 - z

    def dev(z_, y_, x_, c_):
        return (r, ((z_ * 4 + y_) * 4 + x_) * 2 + c_)

    sib = dev(z, y, x, 1 - c)
    zid = dev(zx, y, x, c)
    ids = ((lambda d: dev(z, y, (x + d) % 4, c)), (lambda d: dev(z, (y + d) % 4, x, c)))
    ring_id = ids
    line_id = (ids[1], ids[0])
    p = (x, y)
    q = (y, x)
    w = (wa, wb)
    cols = (slice(0, KW), slice(KW, 2 * KW))
    base = (0, H)
    own, oth = pl.ds(4 * z, 4), pl.ds(4 * zx, 4)
    turn = (1, 3)

    def chunk(g, plane, q_, p_):
        return plane * 16 + (q_ * 4 + p_ if g == 0 else p_ * 4 + q_)

    counts = [0, 0]
    sends = []

    def remote(src, dst, to):
        i = counts[0]
        counts[0] += 1
        cp = pltpu.make_async_remote_copy(
            src_ref=src, dst_ref=dst, send_sem=ssem.at[i], recv_sem=rsem.at[i], device_id=to, device_id_type=MESH
        )
        cp.start()
        sends.append(cp)
        return cp

    def same(ref, to):
        return remote(ref, ref, to)

    def local(src, dst):
        i = counts[1]
        counts[1] += 1
        cp = pltpu.make_async_copy(src, dst, lsem.at[i])
        cp.start()
        return cp

    partners = [sib, zid]
    partners += [ids[0](d) for d in (1, 2, 3)] + [ids[1](d) for d in (1, 2, 3)]
    partners += [((r + d) % 4, f) for d in (1, 2, 3)]
    barrier = pltpu.get_barrier_semaphore()
    for to in partners:
        pl.semaphore_signal(barrier, inc=1, device_id=to, device_id_type=MESH)

    lw_in = local(lw_hbm.at[0], lw)
    lw_in.wait()
    Q = D // 4
    go_in = local(g_hbm.at[0], go)
    xo_in = [local(x_hbm.at[0, :, pl.ds(Q * i, Q)], xo.at[:, pl.ds(Q * i, Q)]) for i in range(4)]
    gw_in = local(gw_hbm, gw)
    om_in = local(om_hbm, om)
    ar_in = local(ar_hbm, ar)
    fragment_in = local(fragment_hbm, fragment)
    for g in range(2):
        w[g][p[g], c, 4 * z + q[g]] = lw[:, cols[g]].astype(BF16)

    pl.semaphore_wait(barrier, len(partners))

    N = 3 * KW // 4
    sib_cols = pl.ds(pl.multiple_of((1 - c) * KW, KW), KW)
    my_cols = pl.ds(pl.multiple_of(c * KW, KW), KW)
    both = range(2)

    def tag(exponent):
        e16 = exponent.astype(I32).astype(I16)
        return jnp.concatenate([e16, e16], axis=0)

    def tag_of(rows):
        return step_of(rows.astype(I32).astype(F32)[0:8])

    def scale_of(bound):
        e = exponent_for(bound)
        return step_of(-e)[0:1], tag(e)

    def largest(values):
        return jnp.broadcast_to(jnp.max(values, axis=(0, 1), keepdims=True), (8, 128))

    def bound_of(g, plane, place):
        tops = [top[chunk(g, plane, k, place)] for k in range(4)]
        return largest(jnp.maximum(jnp.maximum(tops[0], tops[1]), jnp.maximum(tops[2], tops[3])))

    ag0, ag1, ag1x, ag2, ag2x, ag3, ag3x = ([None, None] for _ in range(7))
    cz, so, sx = ([{}, {}] for _ in range(3))

    def cross(g, place):
        return same(w[g].at[place, c, own, :, N:KW], zid)

    def share(g, place, plane):
        return same(w[g].at[place, c, plane], sib)

    def source(g, s):
        return (p[g] + turn[1 - s]) % 4

    def gather_z():
        for g in both:
            ag0[g] = same(w[g].at[p[g], c, 4 * z + q[g], :, 0:N], zid)

    def gather_line():
        for g in both:
            ag1[g] = [same(w[g].at[p[g], c, 4 * z + q[g]], line_id[g](d)) for d in (1, 2, 3)]

    def gather_line_x():
        for g in both:
            ag0[g].wait_recv()
            ag1x[g] = [same(w[g].at[p[g], c, 4 * zx + q[g], :, 0:N], line_id[g](d)) for d in (1, 2, 3)]

    def gather_ring():
        for g in both:
            for cp in ag1[g]:
                cp.wait_recv()
            ag2[g] = [same(w[g].at[p[g], c, own], ring_id[g](turn[s])) for s in both]

    def gather_ring_cross():
        for g in both:
            cz[g][0] = cross(g, p[g])
            so[g][0] = share(g, p[g], own)

    def gather_ring_x():
        for g in both:
            for cp in ag1x[g]:
                cp.wait_recv()
            ag2x[g] = [same(w[g].at[p[g], c, oth, :, 0:N], ring_id[g](turn[s])) for s in both]

    def gather_ring_x_share():
        for g in both:
            cz[g][0].wait_recv()
            sx[g][0] = share(g, p[g], oth)

    def gather_far():
        for g in both:
            ag3[g] = []
            for s in both:
                ag2[g][s].wait_recv()
                src = source(g, s)
                ag3[g].append(same(w[g].at[src, c, pl.ds(4 * z + 2 * s, 2)], ring_id[g](turn[s])))

    def gather_far_cross():
        for g in both:
            for s in both:
                cz[g][1 + s] = cross(g, source(g, s))
                so[g][1 + s] = share(g, source(g, s), own)

    def gather_far_x():
        for g in both:
            ag3x[g] = []
            for s in both:
                ag2x[g][s].wait_recv()
                src = source(g, s)
                ag3x[g].append(same(w[g].at[src, c, pl.ds(4 * zx + 2 * s, 2), :, 0:N], ring_id[g](turn[s])))

    def gather_far_x_share():
        for g in both:
            for s in both:
                cz[g][1 + s].wait_recv()
                sx[g][1 + s] = share(g, source(g, s), oth)

    def gather_end():
        for g in both:
            for s in both:
                ag3[g][s].wait_recv()
            cz[g][3] = cross(g, (p[g] + 2) % 4)
            so[g][3] = share(g, (p[g] + 2) % 4, own)

    def gather_end_x():
        for g in both:
            for s in both:
                ag3x[g][s].wait_recv()
            cz[g][3].wait_recv()
            sx[g][3] = share(g, (p[g] + 2) % 4, oth)

    def multiply(g, place, plane, copy):
        copy.wait_recv()
        parts = []
        rows = []
        lanes = []
        for k in range(4):
            parts += [w[g][place, 0, 4 * plane + k], w[g][place, 1, 4 * plane + k]]
            lanes.append(pl.ds(pl.multiple_of(chunk(g, plane, k, place) * 128, 128), 128))
            rows.append(xo[:, lanes[k]])
        tile = jnp.concatenate(parts, axis=0)
        kva[:, cols[g]] += jnp.dot(jnp.concatenate(rows, axis=1), tile, preferred_element_type=F32)
        back = lax.dot_general(go[:, cols[g]], tile, (((1,), (1,)), ((), ())), preferred_element_type=F32)
        for k in range(4):
            gia[:, lanes[k]] += back[:, 128 * k : 128 * (k + 1)]

    def multiply_own():
        for g in both:
            multiply(g, p[g], z, so[g][0])

    def multiply_own_x():
        for g in both:
            multiply(g, p[g], zx, sx[g][0])

    def multiply_near():
        for g in both:
            for s in both:
                multiply(g, source(g, s), z, so[g][1 + s])

    def multiply_near_x():
        for g in both:
            for s in both:
                multiply(g, source(g, s), zx, sx[g][1 + s])

    def multiply_far():
        for g in both:
            multiply(g, (p[g] + 2) % 4, z, so[g][3])

    def multiply_far_x():
        for g in both:
            multiply(g, (p[g] + 2) % 4, zx, sx[g][3])

    ex = {}

    def exchange():
        ex["g"] = remote(g_hbm.at[0, :, sib_cols], gs, sib)
        ex["x"] = [remote(x_hbm.at[0, :, pl.ds(Q * i, Q)], xs.at[:, pl.ds(Q * i, Q)], sib) for i in range(4)]

    def prepare():
        go_in.wait()
        gt[:, 0:T] = go[:, my_cols].T
        ex["g"].wait_recv()
        gt[:, T:] = gs[...].T
        kva[...] = jnp.zeros_like(kva)
        gia[...] = jnp.zeros_like(gia)

    def gradient(*pieces):
        for i in pieces:
            xo_in[i].wait()
            ex["x"][i].wait_recv()

            def block(n, carry):
                lanes = pl.ds(pl.multiple_of(Q * i + n * 256, 256), 256)
                rows = jnp.concatenate([xo[:, lanes], xs[:, lanes]], axis=0)
                part = jnp.dot(gt[...], rows, preferred_element_type=F32)
                pt[8 * i + 2 * n] = part[:, 0:128]
                pt[8 * i + 2 * n + 1] = part[:, 128:256]
                size = jnp.max(jnp.abs(part).reshape(64, 8, 256), axis=0)
                top[8 * i + 2 * n] = size[:, 0:128]
                top[8 * i + 2 * n + 1] = size[:, 128:256]
                return carry

            lax.fori_loop(0, 4, block, 0, unroll=True)

    stages = (2, 1, 3, 0)
    c1, rs1, rs1x, rs2, rs2x, rs3, rs3x, rs4 = ([None] * 4 for _ in range(8))
    extra = [None] * 4

    def cross_rows(i):
        d = stages[i]
        bound = jnp.maximum(bound_of(0, zx, (p[0] + d) % 4), bound_of(1, zx, (p[1] + d) % 4))
        inv, mark = scale_of(bound)
        for g in both:

            def enc(k, carry, g=g):
                part = pt[chunk(g, zx, k, (p[g] + d) % 4), pl.ds(base[g] + 192, 64)]
                c1s[i, pl.ds(pl.multiple_of(256 * g + 64 * k, 64), 64)] = encode(part, inv)
                return carry

            lax.fori_loop(0, 4, enc, 0)
        c1s[i, 512:528] = mark
        c1[i] = remote(c1s.at[i], c1r.at[i], zid)

    def crossed(i):
        c1[i].wait_recv()
        step = tag_of(c1r[i, 512:528])
        for g in both:

            def add(k, carry, g=g):
                at = chunk(g, z, k, (p[g] + stages[i]) % 4)
                rows = pl.ds(pl.multiple_of(256 * g + 64 * k, 64), 64)
                pt[at, pl.ds(base[g] + 192, 64)] += decode(c1r[i, rows], step[0:1])
                return carry

            lax.fori_loop(0, 4, add, 0)
        extra[stages[i]] = step * TOP

    def hop1(g, s, plane, half, buf, dst, more):
        inv, mark = scale_of(bound_of(g, plane, (p[g] + 2) % 4) + more)

        def enc(k, carry):
            part = pt[chunk(g, plane, k, (p[g] + 2) % 4), pl.ds(base[g] + half * s, half)]
            buf[pl.ds(pl.multiple_of(k * half, half), half)] = encode(part, inv)
            return carry

        lax.fori_loop(0, 4, enc, 0)
        buf[4 * half : 4 * half + 16] = mark
        return remote(buf, dst, ring_id[g](turn[s]))

    def scatter1_x():
        for g in both:
            rs1x[g] = [hop1(g, s, zx, 96, a1xs.at[g, s], a1xr.at[g, s], 0.0) for s in both]

    def scatter1():
        for g in both:
            rs1[g] = [hop1(g, s, z, 128, a1os.at[g, s], a1or.at[g, s], extra[2]) for s in both]

    def hop2(g, s, plane, half, copy, got, buf, dst, more):
        copy.wait_recv()
        step = tag_of(got[4 * half : 4 * half + 16])
        inv, mark = scale_of(more + bound_of(g, plane, (p[g] + turn[s]) % 4) + step * TOP)
        step = step[0:1]

        def enc(k, carry):
            at = chunk(g, plane, k, (p[g] + turn[s]) % 4)
            fed = pt[at, pl.ds(base[g] + half * s, half)] + decode(got[pl.ds(pl.multiple_of(k * half, half), half)], step)
            plain = pt[at, pl.ds(base[g] + half * (1 - s), half)]
            buf[pl.ds(pl.multiple_of(2 * k * half + half * s, half), half)] = encode(fed, inv)
            buf[pl.ds(pl.multiple_of(2 * k * half + half * (1 - s), half), half)] = encode(plain, inv)
            return carry

        lax.fori_loop(0, 4, enc, 0)
        buf[8 * half : 8 * half + 16] = mark
        return remote(buf, dst, ring_id[g](turn[s]))

    def scatter2_x():
        for g in both:
            rs2x[g] = [
                hop2(g, s, zx, 96, rs1x[g][s], a1xr.at[g, s], a2xs.at[g, s], a2xr.at[g, s], 0.0) for s in both
            ]

    def scatter2():
        for g in both:
            rs2[g] = [
                hop2(g, s, z, 128, rs1[g][s], a1or.at[g, s], a2os.at[g, s], a2or.at[g, s], extra[turn[s]]) for s in both
            ]

    def hop3(g, plane, rows, copies, got, buf, dst):
        steps = []
        for s in both:
            copies[s].wait_recv()
            steps.append(tag_of(got[s, 4 * rows : 4 * rows + 16])[0:1])
        size = jnp.zeros((8, 128), F32)
        for d in (1, 2, 3, 0):
            k = (q[g] + d) % 4
            part = pl.ds(pl.multiple_of(k * rows, rows), rows)
            at = chunk(g, plane, k, p[g])
            total = pt[at, pl.ds(base[g], rows)] + decode(got[0, part], steps[0]) + decode(got[1, part], steps[1])
            pt[at, pl.ds(base[g], rows)] = total
            if d:
                size = jnp.maximum(size, jnp.max(jnp.abs(total).reshape(rows // 8, 8, 128), axis=0))
        inv, mark = scale_of(largest(size))
        sent = []
        for d in (1, 2, 3):
            at = chunk(g, plane, (q[g] + d) % 4, p[g])
            buf[d - 1, 0:rows] = encode(pt[at, pl.ds(base[g], rows)], inv)
            buf[d - 1, rows : rows + 16] = mark
            sent.append(remote(buf.at[d - 1], dst.at[d - 1], line_id[g](d)))
        return sent

    def scatter3_x():
        for g in both:
            rs3x[g] = hop3(g, zx, 192, rs2x[g], a2xr.at[g], a3xs.at[g], a3xr.at[g])

    def scatter3():
        for g in both:
            rs3[g] = hop3(g, z, 256, rs2[g], a2or.at[g], a3os.at[g], a3or.at[g])

    def scatter4():
        for g in both:
            part = pt[chunk(g, zx, q[g], p[g]), pl.ds(base[g], 192)]
            for j in range(3):
                rs3x[g][j].wait_recv()
                part = part + decode(a3xr[g, j, 0:192], tag_of(a3xr[g, j, 192:208])[0:1])
            inv, mark = scale_of(largest(jnp.abs(part)))
            a4s[g, 0:192] = encode(part, inv)
            a4s[g, 192:208] = mark
            rs4[g] = remote(a4s.at[g], a4r.at[g], zid)

    def scatter_end():
        for g in both:
            part = pt[chunk(g, z, q[g], p[g]), pl.ds(base[g], 256)]
            for j in range(3):
                rs3[g][j].wait_recv()
                part = part + decode(a3or[g, j, 0:256], tag_of(a3or[g, j, 256:272])[0:1])
            acc[pl.ds(base[g], 256)] = part
            rs4[g].wait_recv()
            acc[pl.ds(base[g], 192)] += decode(a4r[g, 0:192], tag_of(a4r[g, 192:208])[0:1])
            gr[:, pl.ds(base[g], 256)] = acc[pl.ds(base[g], 256)].T
        ex["gx"] = remote(gr.at[pl.ds(pl.multiple_of((1 - c) * 64, 64), 64)], gx, sib)

    def is_first():
        return fragment[0] % 2 == 0

    def delta():
        gw_in.wait()
        fragment_in.wait()
        first = is_first()
        dl[...] = jnp.where(first, gw[:, 0:KW] - lw[:, 0:KW], gw[:, KW:] - lw[:, KW:])
        ed = exponent_for(largest(jnp.abs(dl[...])))
        ds[0:64] = encode(dl[...], jnp.concatenate([step_of(-ed)[0:1]] * 4, axis=1))
        ds[64:80] = jnp.concatenate([tag(ed)] * 4, axis=1)

    def replicas():
        ex["rep"] = [remote(ds, dr.at[d - 1], ((r + d) % 4, f)) for d in (1, 2, 3)]

    def outer():
        om_in.wait()
        first = is_first()
        mean_delta = dl[...]
        for j in range(3):
            ex["rep"][j].wait_recv()
            step = tag_of(dr[j, 64:80])
            mean_delta = mean_delta + decode(dr[j, 0:64], step[0:1])
        mean_delta = mean_delta * 0.25
        moment_new = moment_keep * jnp.where(first, om[:, 0:KW], om[:, KW:]) + mean_delta
        global_new = jnp.where(first, gw[:, 0:KW], gw[:, KW:]) - outer_rate * (mean_delta + moment_keep * moment_new)
        for h in both:
            sel = first if h == 0 else jnp.logical_not(first)
            mno[:, cols[h]] = jnp.where(sel, moment_new, om[:, cols[h]])
            gno[:, cols[h]] = jnp.where(sel, global_new, gw[:, cols[h]])

    def half_out(plane):
        lanes = pl.ds(pl.multiple_of(plane * (D // 2), D // 2), D // 2)
        gio[:, lanes] = gia[:, lanes].astype(BF16)

    def products_own():
        half_out(z)

    def products_x():
        half_out(zx)
        kvo[...] = kva[...].astype(BF16)

    def inner_out():
        ar_in.wait()
        ex["gx"].wait_recv()
        first = is_first()
        here = gr[pl.ds(pl.multiple_of(c * 64, 64), 64)]
        there = gx[...]
        for h in both:
            gradient_h = jnp.where(c == h, here, there)
            inner = lw[:, cols[h]] - inner_rate * gradient_h
            sel = first if h == 0 else jnp.logical_not(first)
            merged = merge_keep * inner + (1.0 - merge_keep) * ar[...]
            lno[:, cols[h]] = jnp.where(sel, merged, inner)

    gather_z()
    gather_line()
    exchange()
    delta()
    prepare()
    gather_line_x()
    gather_ring()
    gather_ring_cross()
    gradient(0,1,2,3)
    for i in range(4):
        cross_rows(i)
    scatter1_x()
    gather_ring_x()
    crossed(0)
    scatter1()
    gather_ring_x_share()
    scatter2_x()
    replicas()
    multiply_own()
    crossed(1)
    crossed(2)
    scatter2()
    gather_far()
    gather_far_cross()
    multiply_own_x()
    scatter3_x()
    gather_far_x()
    gather_far_x_share()
    crossed(3)
    scatter3()
    outer()
    multiply_near()
    gather_end()
    scatter4()
    multiply_near_x()
    multiply_far()
    products_own()
    gather_end_x()
    scatter_end()
    multiply_far_x()
    products_x()
    inner_out()

    for cp in sends:
        cp.wait_send()
    assert counts[0] <= N_REMOTE and counts[1] <= N_LOCAL


def write_out(*refs):
    sem = refs[10]
    copies = [pltpu.make_async_copy(refs[i], refs[5 + i], sem.at[i]) for i in range(5)]
    for cp in copies:
        cp.start()
    for cp in copies:
        cp.wait()


N_REMOTE = 120
N_LOCAL = 16


def device_step(inputs, grad_kv, local_weight, global_weight, outer_moment, arrived, fragment):
    hbm = pl.BlockSpec(memory_space=pltpu.HBM)
    vmem = pl.BlockSpec(memory_space=pltpu.VMEM)
    R = D // 64
    V = pltpu.VMEM
    shapes = (((T, 2 * KW), BF16), ((T, D), BF16), ((R, 2 * KW), F32), ((R, 2 * KW), F32), ((R, 2 * KW), F32))
    held = pl.pallas_call(
        kernel,
        out_shape=tuple(V(shape, dtype) for shape, dtype in shapes),
        in_specs=[hbm] * 7,
        out_specs=[vmem] * 5,
        scratch_shapes=[
            V((T, D), BF16), V((T, D), BF16),
            V((T, 2 * KW), BF16), V((T, KW), BF16), V((KW, 2 * T), BF16),
            V((R, 2 * KW), F32), V((R, 2 * KW), F32), V((R, 2 * KW), F32), V((R, KW), F32),
            V((4, 2, 8, R, KW), BF16), V((4, 2, 8, R, KW), BF16),
            V((32, KW, 128), F32), V((32, 8, 128), F32),
            V((4, 528, 128), I16), V((4, 528, 128), I16),
            V((2, 2, 528, 128), I16), V((2, 2, 528, 128), I16),
            V((2, 2, 400, 128), I16), V((2, 2, 400, 128), I16),
            V((2, 2, 1040, 128), I16), V((2, 2, 1040, 128), I16),
            V((2, 2, 784, 128), I16), V((2, 2, 784, 128), I16),
            V((2, 3, 272, 128), I16), V((2, 3, 272, 128), I16),
            V((2, 3, 208, 128), I16), V((2, 3, 208, 128), I16),
            V((2, 208, 128), I16), V((2, 208, 128), I16),
            V((KW, 128), F32), V((T, 2 * KW), F32), V((T, D), F32),
            V((128, KW), F32), V((R, KW), F32), V((R, KW), F32),
            V((R + 16, KW), I16), V((3, R + 16, KW), I16),
            pltpu.SMEM((1,), I32),
            pltpu.SemaphoreType.DMA((N_LOCAL,)),
            pltpu.SemaphoreType.DMA((N_REMOTE,)),
            pltpu.SemaphoreType.DMA((N_REMOTE,)),
        ],
        compiler_params=pltpu.CompilerParams(
            collective_id=0, has_side_effects=True, vmem_limit_bytes=60 * 1024 * 1024
        ),
        name="step",
    )(fragment, inputs, grad_kv, local_weight, global_weight, outer_moment, arrived)
    kv, gi, ln, gn, mn = pl.pallas_call(
        write_out,
        out_shape=tuple(jax.ShapeDtypeStruct(shape, dtype) for shape, dtype in shapes),
        in_specs=[vmem] * 5,
        out_specs=[hbm] * 5,
        scratch_shapes=[pltpu.SemaphoreType.DMA((5,))],
        compiler_params=pltpu.CompilerParams(vmem_limit_bytes=1024 * 1024),
        name="write",
    )(*(pltpu.with_memory_space_constraint(a, pltpu.VMEM) for a in held))
    return kv[None], gi[None], ln[None], gn, mn


def solution(mesh):
    return jax.shard_map(
        device_step,
        mesh=mesh,
        in_specs=(
            P("rep", "fsdp", None),
            P("rep", "fsdp", None),
            P("rep", "fsdp", None),
            P("fsdp", None),
            P("fsdp", None),
            P("fsdp", None),
            P(),
        ),
        out_specs=(
            P("rep", "fsdp", None),
            P("rep", "fsdp", None),
            P("rep", "fsdp", None),
            P("fsdp", None),
            P("fsdp", None),
        ),
        check_vma=False,
    )
```

time: 456 us -> 61.1 us (0.13)
  waiting for transfers between devices: 409 us -> 0 us
  Pallas kernels: 0 us -> 59.7 us
  matrix products: 19.2 us -> 0 us
  between operations: 16.2 us -> 1.29 us
  other arithmetic: 5.17 us -> 0 us
    reduce_scatter x1 -> x0, waiting for transfers between devices: 300 us -> none  [local(): lax.psum_scatter(lax.dot_general(rows, cotangent, contract_rows, preferre...]
    all_gather x1 -> x0, waiting for transfers between devices: 68 us -> none  [local(): full_weight = lax.all_gather(weight_bf, 'fsdp', axis=0, tiled=True)]
    pallas_call x0 -> x2, Pallas kernels: none -> 59.7 us  [the longest x1 58.1 us: device_step(): pl.pallas_call(kernel, out_shape=tuple((V(shape, dtype) for shape, dtype...]
    psum x1 -> x0, waiting for transfers between devices: 41.4 us -> none  [local(): delta_sum = lax.psum(delta, 'rep')]
    dot_general x3 -> x0, matrix products: 19.2 us -> none  [the longest x1 9.11 us: local(): lax.dot_general(rows, cotangent, contract_rows, preferred_element_type=jn...]
  transfers between devices with their start and end apart: 3 -> 0, of which waited for: 3 -> 0; matrix products, arithmetic and copies ran while one was open for 5% -> 0% of each run, Pallas kernels for 0% -> 0%
where the time goes in v3:
time: 61.1 us; the launch traced here: 61 us
  Pallas kernels  59.7 us (98%)
  between operations  1.29 us (2%)
    pallas_call x1, Pallas kernels, device_step(): pl.pallas_call(kernel, out_shape=tuple((V(shape, dtype) for shape, dtype...  58.1 us
    pallas_call x1, Pallas kernels, device_step(): pl.pallas_call(write_out, out_shape=tuple((jax.ShapeDtypeStruct(shape, dt...  1.57 us

profile of v3, /device:TPU:1, one launch (start us, length us, event | category | flops | bytes accessed | tf_op | source)
XLA Modules:
  0.0 61.0 jit_solution(16708881909758223783)
XLA Ops:
  1.3 58.1 %step.1 = (bf16[192,1024]{1,0:T(8,128)(2,1)S(1)}, bf16[192,4096]{1,0:T(8,128)(2,1)S(1)}, f32[64,1024]{1,0:T(8,128)S(1)}, f32[64,1024]{1,0:T(8,128)S(1)}, f32[64,1024]{1,0:T(8,128)S(1)}) custom-call(s32[1]{0:T(128)S(6)} %copy.12.fragment_hbm, bf16[1,192,4096]{2,1,0:T(8,128)(2,1)} %x_hbm.1, bf16[1,192,1024]{2,1,0:T(8,128)(2,1)} %g_hbm.1, ...), custom_call_target="tpu_custom_call" | custom-call | tf_op jit(solution)/shard_map/step/pallas_call | solution.py:559
  59.4 1.6 %write.1 = (bf16[192,1024]{1,0:T(8,128)(2,1)}, bf16[192,4096]{1,0:T(8,128)(2,1)}, f32[64,1024]{1,0:T(8,128)}, f32[64,1024]{1,0:T(8,128)}, f32[64,1024]{1,0:T(8,128)}) custom-call(bf16[192,1024]{1,0:T(8,128)(2,1)S(1)} %get-tuple-element.15.refs_0_, bf16[192,4096]{1,0:T(8,128)(2,1)S(1)} %get-tuple-element.16.refs_1_, ...), custom_call_target="tpu_custom_call" | custom-call | tf_op jit(solution)/shard_map/write/pallas_call | solution.py:591

commit v4 on v3

--- a/solution.py
+++ b/solution.py
@@ -99,6 +99,8 @@
         pl.semaphore_signal(barrier, inc=1, device_id=to, device_id_type=MESH)
 
     lw_in = local(lw_hbm.at[0], lw)
+    kva[...] = jnp.zeros_like(kva)
+    gia[...] = jnp.zeros_like(gia)
     lw_in.wait()
     Q = D // 4
     go_in = local(g_hbm.at[0], go)
@@ -276,8 +278,6 @@
         gt[:, 0:T] = go[:, my_cols].T
         ex["g"].wait_recv()
         gt[:, T:] = gs[...].T
-        kva[...] = jnp.zeros_like(kva)
-        gia[...] = jnp.zeros_like(gia)
 
     def gradient(*pieces):
         for i in pieces:
@@ -492,7 +492,6 @@
     gather_z()
     gather_line()
     exchange()
-    delta()
     prepare()
     gather_line_x()
     gather_ring()
@@ -506,6 +505,7 @@
     scatter1()
     gather_ring_x_share()
     scatter2_x()
+    delta()
     replicas()
     multiply_own()
     crossed(1)

time: 61.1 us -> 61.1 us (level)
  no operation moved by 1% of the time
where the time goes in v4:
time: 61.1 us; the launch traced here: 61 us
  Pallas kernels  59.7 us (98%)
  between operations  1.29 us (2%)
    pallas_call x1, Pallas kernels, device_step(): pl.pallas_call(kernel, out_shape=tuple((V(shape, dtype) for shape, dtype...  58.1 us
    pallas_call x1, Pallas kernels, device_step(): pl.pallas_call(write_out, out_shape=tuple((jax.ShapeDtypeStruct(shape, dt...  1.57 us

profile of v4, /device:TPU:1, one launch (start us, length us, event | category | flops | bytes accessed | tf_op | source)
XLA Modules:
  0.0 61.0 jit_solution(16680544311932921182)
XLA Ops:
  1.3 58.1 %step.1 = (bf16[192,1024]{1,0:T(8,128)(2,1)S(1)}, bf16[192,4096]{1,0:T(8,128)(2,1)S(1)}, f32[64,1024]{1,0:T(8,128)S(1)}, f32[64,1024]{1,0:T(8,128)S(1)}, f32[64,1024]{1,0:T(8,128)S(1)}) custom-call(s32[1]{0:T(128)S(6)} %copy.12.fragment_hbm, bf16[1,192,4096]{2,1,0:T(8,128)(2,1)} %x_hbm.1, bf16[1,192,1024]{2,1,0:T(8,128)(2,1)} %g_hbm.1, ...), custom_call_target="tpu_custom_call" | custom-call | tf_op jit(solution)/shard_map/step/pallas_call | solution.py:559
  59.4 1.6 %write.1 = (bf16[192,1024]{1,0:T(8,128)(2,1)}, bf16[192,4096]{1,0:T(8,128)(2,1)}, f32[64,1024]{1,0:T(8,128)}, f32[64,1024]{1,0:T(8,128)}, f32[64,1024]{1,0:T(8,128)}) custom-call(bf16[192,1024]{1,0:T(8,128)(2,1)S(1)} %get-tuple-element.15.refs_0_, bf16[192,4096]{1,0:T(8,128)(2,1)S(1)} %get-tuple-element.16.refs_1_, ...), custom_call_target="tpu_custom_call" | custom-call | tf_op jit(solution)/shard_map/write/pallas_call | solution.py:591
